TPU v7x, 32 devices: a whole 2x2x4 slice. The times are simulated.
32 devices in a mesh: groups: 2 (over x), tp: 16 (over z, y, core).
Axes of the slice: x: 2, y: 2, z: 4, core: 2. Of those that a mesh axis runs over, the one named last changes fastest.
Arguments:
- residual: bfloat16 [2, 8, 16384], P(None, 'groups', 'tp'), parts along dimension 1, may hold values from -4 to 4, as said below
- norm_gain: bfloat16 [16384], P('tp'), may hold values from 0.099609375 to 1.8984375
- w_query: bfloat16 [16384, 8192], P('tp'), may hold values from -0.046875 to 0.046875
- w_keyval: bfloat16 [16384, 2048], P('tp'), may hold values from -0.046875 to 0.046875
- w_out: bfloat16 [8192, 16384], P('tp'), may hold values from -0.75 to 0.75
- kv_cache: bfloat16 [8, 4096, 2048], P('groups', 'tp'), parts along dimension 0, may hold values from -103 to 103
- lengths: int32 [8], P('groups'), parts along dimension 0, may hold values from 1 to 4096, 8192 in all
Outputs:
- hidden_out: bfloat16 [2, 8, 16384], P(None, 'groups', 'tp'), parts along dimension 1
There are 2 independent parts, one for each index of `groups`. A program takes and returns all parts, laid end to end along the dimension named above; an argument that names none is the same for every part. Nothing has to cross between parts.
Inputs may be any that keep to these rules, and one draw needn't show every extreme that they name: `residual`: the layer's input rows. `lengths`: some row fills all 4096 cache positions.
All inputs are finite; a program needn't handle non-finite values.
Results may differ from a plain program's by a relative error of at most 0.015.
The roundings to bfloat16 on the way count: a program that leaves them out, or rounds other values in their place, can miss the bound.
Values may be sent and summed in bfloat16 or wider, within the bound.
A program may use at most 128 MiB of HBM per device.

v0:
```python
import jax
import jax.numpy as jnp
from jax import lax
from jax.sharding import PartitionSpec as P

D = 16384
QH = 64
KVH = 8
HD = 128


def rotate(vectors, position):
    halfway = vectors.shape[-1] // 2
    frequency = 500000.0 ** (-2.0 * jnp.arange(halfway, dtype=jnp.float32) / vectors.shape[-1])
    angles = position[..., None, None].astype(jnp.float32) * frequency
    cosine = jnp.cos(angles)
    sine_part = jnp.sin(angles)
    leading = vectors[..., :halfway]
    trailing = vectors[..., halfway:]
    return jnp.concatenate(
        [leading * cosine - trailing * sine_part, trailing * cosine + leading * sine_part], axis=-1
    )


def on_device(residual, norm_gain, w_query, w_keyval, w_out, kv_cache, lengths):
    step_count, row_count, local_width = residual.shape
    ranks = lax.axis_size("tp")
    device_rank = lax.axis_index("tp")
    head_local = QH // ranks
    group_size = QH // KVH
    window = kv_cache.shape[1]
    inv_root = HD ** (-0.5)
    wide_residual = residual.astype(jnp.float32)
    squares = lax.psum(jnp.sum(wide_residual * wide_residual, axis=-1), "tp")
    scaling = lax.rsqrt(squares / D + 1e-05)
    normed = (wide_residual * scaling[..., None] * norm_gain.astype(jnp.float32)).astype(
        jnp.bfloat16
    )
    flat_rows = normed.reshape(step_count * row_count, local_width)
    query_part = jnp.dot(flat_rows, w_query, preferred_element_type=jnp.float32)
    keyval_part = jnp.dot(flat_rows, w_keyval, preferred_element_type=jnp.float32)
    position = lengths[None, :] + jnp.arange(step_count, dtype=jnp.int32)[:, None]
    query_total, keyval_total = lax.psum((query_part, keyval_part), "tp")
    queries = rotate(query_total.reshape(step_count, row_count, QH, HD), position).astype(
        jnp.bfloat16
    )
    queries = queries.reshape(step_count, row_count, KVH, group_size, HD)
    keyval_total = keyval_total.reshape(step_count, row_count, 2, KVH, HD)
    new_keys = rotate(keyval_total[:, :, 0], position).astype(jnp.bfloat16)
    new_values = keyval_total[:, :, 1].astype(jnp.bfloat16)
    cache_keys = kv_cache[:, :, : KVH * HD].reshape(row_count, window, KVH, HD)
    cache_values = kv_cache[:, :, KVH * HD :].reshape(row_count, window, KVH, HD)
    slots = device_rank * window + jnp.arange(window, dtype=jnp.int32)
    valid = slots[None, :] < lengths[:, None]
    live_slots = valid[None, :, None, None, :]
    cached = (
        jnp.einsum("srkgd,rlkd->srkgl", queries, cache_keys, preferred_element_type=jnp.float32)
        * inv_root
    )
    cached = jnp.where(live_slots, cached, -1e30)
    local_top = jnp.max(cached, axis=-1)
    cache_weights = jnp.where(live_slots, jnp.exp(cached - local_top[..., None]), 0.0).astype(
        jnp.bfloat16
    )
    cache_total = jnp.sum(cache_weights.astype(jnp.float32), axis=-1)
    cache_out = jnp.einsum(
        "srkgl,rlkd->srkgd", cache_weights, cache_values, preferred_element_type=jnp.float32
    )
    fresh = (
        jnp.einsum("srkgd,urkd->srkgu", queries, new_keys, preferred_element_type=jnp.float32)
        * inv_root
    )
    causal = jnp.arange(step_count)[:, None] >= jnp.arange(step_count)[None, :]
    fresh = jnp.where(causal[:, None, None, None, :], fresh, -1e30)
    cache_top = lax.pmax(local_top, "tp")
    top = jnp.maximum(cache_top, jnp.max(fresh, axis=-1))
    rescale = jnp.exp(local_top - top)
    scaled_out = (cache_out * rescale[..., None]).reshape(step_count, row_count, QH * HD)
    scaled_total = (cache_total * rescale).reshape(step_count, row_count, QH)
    out_mine = lax.psum_scatter(scaled_out, "tp", scatter_dimension=2, tiled=True)
    total_every = lax.psum(scaled_total, "tp")
    total_mine = lax.dynamic_slice_in_dim(total_every, device_rank * head_local, head_local, 2)
    fresh_weights = jnp.exp(fresh - top[..., None]).astype(jnp.bfloat16)
    fresh_total = jnp.sum(fresh_weights.astype(jnp.float32), axis=-1).reshape(
        step_count, row_count, QH
    )
    fresh_out = jnp.einsum(
        "srkgu,urkd->srkgd", fresh_weights, new_values, preferred_element_type=jnp.float32
    )
    fresh_out = fresh_out.reshape(step_count, row_count, QH * HD)
    fresh_out_mine = lax.dynamic_slice_in_dim(
        fresh_out, device_rank * head_local * HD, head_local * HD, 2
    )
    fresh_total_mine = lax.dynamic_slice_in_dim(
        fresh_total, device_rank * head_local, head_local, 2
    )
    denominators = total_mine + fresh_total_mine
    numerators = (out_mine + fresh_out_mine).reshape(step_count, row_count, head_local, HD)
    attended = (numerators / denominators[..., None]).astype(jnp.bfloat16)
    attended = attended.reshape(step_count * row_count, head_local * HD)
    partial_value = jnp.dot(attended, w_out, preferred_element_type=jnp.float32)
    partial_value = partial_value.reshape(step_count, row_count, w_out.shape[1])
    summed = lax.psum_scatter(
        partial_value.astype(jnp.bfloat16), "tp", scatter_dimension=2, tiled=True
    ).astype(jnp.float32)
    return (wide_residual + summed).astype(jnp.bfloat16)


def solution(mesh):
    placed = (
        P(None, "groups", "tp"),
        P("tp"),
        P("tp", None),
        P("tp", None),
        P("tp", None),
        P("groups", "tp", None),
        P("groups"),
    )
    return jax.shard_map(
        on_device, mesh=mesh, in_specs=placed, out_specs=P(None, "groups", "tp"), check_vma=False
    )
```

profile of v0, /device:TPU:0, one launch (start us, length us, event | category | flops | bytes accessed | tf_op | source)
XLA Modules:
  0.0 408.6 jit_solution(17346266538369549003)
XLA Ops:
  6.5 0.8 fusion.10
  7.4 0.7 convert_element_type.52
  8.0 34.9 %psum.28 = f32[2,4]{1,0:T(2,128)S(1)} all-reduce(f32[2,4]{1,0:T(2,128)S(1)} %fusion.10), channel_id=1, replica_groups=mesh['groups'=2,'tp'=16] {'tp'}, use_global_device_ids=true, to_apply=%region_1.0 | all-reduce | flops 8 | bytes 64 | tf_op jit(solution)/shard_map/psum | solution.py:34
  42.9 0.8 fusion.12
  43.8 8.2 %convolution_bitcast_fusion.1 = f32[1,8,64,128]{3,1,2,0:T(8,128)S(1)} fusion(bf16[8,1024]{1,0:T(8,128)(2,1)S(1)} %reshape.122, bf16[1024,8192]{1,0:T(8,128)(2,1)} %param.9), kind=kOutput, calls=%fused_computation.7 | convolution fusion | flops 134217728 | bytes 17055744 | tf_op jit(solution)/shard_map/dot_general | solution.py:40
  52.0 0.8 copy.67
  52.7 0.7 convolution_bitcast_fusion.3
  53.4 0.7 copy.45
  54.2 4.6 %fusion.24 = (bf16[4,256,1024]{2,1,0:T(8,128)(2,1)}, bf16[4,256,1024]{2,1,0:T(8,128)(2,1)}) fusion(bf16[4,256,2048]{2,1,0:T(8,128)(2,1)} %param.12), kind=kLoop, calls=%fused_computation.55 | loop fusion | bytes 8388608 | tf_op jit(solution)/shard_map/slice | solution.py:52
  59.1 2.9 copy.65
  62.0 4.0 copy.66
  66.0 74.2 %all-reduce.3.cloned.1.call-done = (f32[2,4,64,128]{3,2,1,0:T(8,128)}, f32[2,4,2,8,128]{4,0,3,1,2:T(2,128)}) async-done(((f32[2,4,64,128]{3,2,1,0:T(8,128)}, f32[2,4,2,8,128]{4,0,3,1,2:T(2,128)}), (f32[2,4,64,128]{3,2,1,0:T(8,128)}, f32[2,4,2,8,128]{4,0,3,1,2:T(2,128)})) %all-reduce.3.cloned.1.call-update) | async-done | bytes 327696 | tf_op jit(solution)/shard_map/psum | solution.py:43
  140.1 0.8 slice_bitcast_fusion
  141.0 1.2 fusion.6
  142.2 0.5 fusion.25
  142.7 60.5 %pmax.7 = f32[2,4,8,8]{3,0,2,1:T(2,128)S(1)} all-reduce(f32[2,4,8,8]{3,0,2,1:T(2,128)S(1)} %get-tuple-element.18), channel_id=1, replica_groups=mesh['groups'=2,'tp'=16] {'tp'}, use_global_device_ids=true, to_apply=%region_4.5 | all-reduce | flops 512 | bytes 4096 | tf_op jit(solution)/shard_map/pmax | solution.py:75
  203.2 0.3 convert_reduce_fusion
  203.5 0.8 fusion.26
  204.3 2.3 fusion.3
  206.6 5.9 %copy.63 = f32[2,4,8,8,128]{1,0,4,3,2:T(2,128)} copy(f32[2,4,8,8,128]{4,3,0,2,1:T(8,128)S(1)} %fusion.3) | data formatting | bytes 524288
  212.5 8.8 %reshape.136 = f32[8192,8]{1,0:T(8,128)} reshape(f32[8192,2,4]{2,1,0:T(2,128)} %bitcast.77) | data formatting | bytes 524288
  221.7 29.7 %psum.31 = f32[2,4,64]{2,1,0:T(4,128)S(1)} all-reduce(f32[2,4,64]{2,1,0:T(4,128)S(1)} %reshape.129), channel_id=1, replica_groups=mesh['groups'=2,'tp'=16] {'tp'}, use_global_device_ids=true, to_apply=%region_9.10 | all-reduce | flops 512 | bytes 4096 | tf_op jit(solution)/shard_map/psum | solution.py:81
  251.6 0.2 convolution_bitcast_fusion.2
  252.0 39.0 %reduce-scatter.7.cloned.1.call-done = f32[512,8]{1,0:T(8,128)} async-done(((f32[8192,8]{1,0:T(8,128)}), f32[512,8]{1,0:T(8,128)}) %reduce-scatter.7.cloned.1.call-update) | async-done | bytes 16400
  291.0 1.3 reshape.137
  292.5 8.2 %convolution_convert_fusion = bf16[2,4,16384]{2,1,0:T(4,128)(2,1)S(1)} fusion(bf16[512,16384]{1,0:T(8,128)(2,1)} %param.11, f32[2,4,512]{2,1,0:T(4,128)S(1)} %div.25, f32[2,4,512]{2,1,0:T(4,128)S(1)} %copy.60, f32[2,4,8192]{2,1,0:T(4,128)S(1)} %reshape.128, s32[]{:T(128)S(6)} %select_n.25), kind=kOutput, calls=%fused_computation | convolution fusion | flops 134361088 | bytes 17088516 | tf_op jit(solution)/shard_map/dot_general | solution.py:101
  300.7 13.0 %copy.61 = bf16[2,4,16384]{1,0,2:T(2,128)(2,1)} copy(bf16[2,4,16384]{2,1,0:T(4,128)(2,1)S(1)} %convolution_convert_fusion) | data formatting | bytes 524288
  313.7 14.2 %reshape.138 = bf16[16384,8]{1,0:T(8,128)(2,1)} reshape(bf16[16384,2,4]{2,1,0:T(2,128)(2,1)} %bitcast.78) | data formatting | bytes 524288
  327.9 72.0 %reduce-scatter.9.cloned.1.call-done = bf16[1024,8]{1,0:T(8,128)(2,1)} async-done(((bf16[16384,8]{1,0:T(8,128)(2,1)}), bf16[1024,8]{1,0:T(8,128)(2,1)}) %reduce-scatter.9.cloned.1.call-update) | async-done | bytes 16400
  399.8 1.2 reshape.139
  401.0 0.4 copy.62
  401.4 0.6 fusion.13
  (38 shorter events, 1.4 us)
Async XLA Ops:
  6.5 133.6 %all-reduce.3.cloned.1.call-start = ((), (), s32[]{:S(2)}) async-start(), calls=%async_computation.4 | async-start | bytes 655360 | tf_op jit(solution)/shard_map/psum | solution.py:43
  43.8 9.0 %copy-start = (bf16[1024,2048]{1,0:T(8,128)(2,1)S(1)}, bf16[1024,2048]{1,0:T(8,128)(2,1)}, u32[]{:S(2)}) copy-start(bf16[1024,2048]{1,0:T(8,128)(2,1)} %param.10) | copy-start | bytes 12582916
  52.0 2.2 copy-start.3
  54.1 236.9 %reduce-scatter.7.cloned.1.call-start = ((), (), s32[]{:S(2)}) async-start(), calls=%async_computation.2 | async-start | bytes 4456448
  221.3 30.3 %copy-start.2 = (f32[2,4,2,8,128]{4,0,3,1,2:T(2,128)S(1)}, f32[2,4,2,8,128]{4,0,3,1,2:T(2,128)}, u32[]{:S(2)}) copy-start(f32[2,4,2,8,128]{4,0,3,1,2:T(2,128)} %get-tuple-element.6) | copy-start | bytes 196612
  221.3 178.5 %reduce-scatter.9.cloned.1.call-start = ((), (), s32[]{:S(2)}) async-start(), calls=%async_computation.3 | async-start | bytes 4456448
  327.9 73.6 %copy-start.1 = (bf16[2,4,1024]{2,1,0:T(4,128)(2,1)S(1)}, bf16[2,4,1024]{2,1,0:T(4,128)(2,1)}, u32[]{:S(2)}) copy-start(bf16[2,4,1024]{2,1,0:T(4,128)(2,1)} %param.7) | copy-start | bytes 49156
Sparse Core Ops, SparseCore 0:
  54.2 85.8 all-reduce.2
  221.5 69.5 reduce-scatter.6
  328.0 71.7 reduce-scatter.8
where the time goes:
time: 410 us; the launch traced here: 409 us
  waiting for transfers between devices  185 us (45%)
  blocking collectives  125 us (30%)
  local copies, waits for them, and re-layouts  59 us (14%)
  matrix products  20.9 us (5%)
  between operations  13.3 us (3%)
  other arithmetic  5.05 us (1%)
    unnamed x5, waiting for transfers between devices  111 us
    psum x1, waiting for transfers between devices, on_device(): query_total, keyval_total = lax.psum((query_part, keyval_part), 'tp')  74.2 us
    pmax x1, blocking collectives, on_device(): cache_top = lax.pmax(local_top, 'tp')  60.5 us
    unnamed x20, local copies, waits for them, and re-layouts  52.5 us
    psum x1, blocking collectives, on_device(): squares = lax.psum(jnp.sum(wide_residual * wide_residual, axis=-1), 'tp')  34.9 us
    psum x1, blocking collectives, on_device(): total_every = lax.psum(scaled_total, 'tp')  29.7 us
  transfers between devices with their start and end apart: 3, of which 3 were waited for; matrix products, arithmetic and copies ran while one was open for 3% of the time, Pallas kernels for 0%

commit v1 on v0

v1 whole, which is shorter than its diff:
```python
import functools

import jax
import jax.numpy as jnp
from jax import lax
from jax.experimental import pallas as pl
from jax.experimental.pallas import tpu as pltpu
from jax.sharding import PartitionSpec as P

QH = 64
KVH = 8
HD = 128
UNITS = 2 * KVH
GROUP = QH // KVH
LIVE_MIN = -1e30
MESH = pl.DeviceIdType.MESH
SQ, QKV, GATHER, MERGE, PROJ = range(5)


def kernel(
    n,
    len_ref, res_ref, gain_ref, cos_ref, sin_ref, wq_hbm, wkv_hbm, wo_hbm, kv_hbm,
    out_ref,
    wq_v, wkv_v, wo_v, kv_v, sq_buf, kv_part, q_send, q_recv, gathered,
    o_send, o_recv, p_send, p_recv,
    wq_sem, wkv_sem, wo_sem, kv_sem, send_sem, recv_sem,
):
    steps, requests, width = res_ref.shape
    rows = steps * requests
    window = kv_hbm.shape[1]
    features = width * n
    heads = QH // n
    columns = heads * HD
    head_rows = heads * rows
    per_kv = n // KVH
    per_unit = n // UNITS
    me = lax.axis_index("tp")

    def peer_at(i):
        return lax.rem(me + i, n)

    def source_at(i):
        return lax.rem(me - i + n, n)

    def remote(phase, i, src, dst, peer):
        return pltpu.make_async_remote_copy(
            src_ref=src,
            dst_ref=dst,
            send_sem=send_sem.at[phase, i],
            recv_sem=recv_sem.at[phase, i],
            device_id={"tp": peer},
            device_id_type=MESH,
        )

    def each_peer(body):
        lax.fori_loop(1, n, lambda i, c: (body(i), c)[1], 0)

    def wq_copy(i):
        at = pl.multiple_of(peer_at(i) * columns, columns)
        return pltpu.make_async_copy(wq_hbm.at[:, pl.ds(at, columns)], wq_v.at[i], wq_sem.at[i])

    def wo_copy(i):
        at = pl.multiple_of(peer_at(i) * width, width)
        return pltpu.make_async_copy(wo_hbm.at[:, pl.ds(at, width)], wo_v.at[i], wo_sem.at[i])

    wkv_copy = pltpu.make_async_copy(wkv_hbm, wkv_v, wkv_sem)
    kv_copy = pltpu.make_async_copy(kv_hbm, kv_v, kv_sem)
    wkv_copy.start()
    each_peer(lambda i: wq_copy(i).start())
    wq_copy(0).start()

    barrier = pltpu.get_barrier_semaphore()
    each_peer(
        lambda i: pl.semaphore_signal(
            barrier, inc=1, device_id={"tp": peer_at(i)}, device_id_type=MESH
        )
    )
    residual = jnp.concatenate(
        [res_ref[s].astype(jnp.float32) for s in range(steps)], axis=0
    )
    sq_buf[me] = jnp.broadcast_to(
        jnp.sum(residual * residual, axis=-1, keepdims=True), (rows, HD)
    )
    pl.semaphore_wait(barrier, n - 1)

    each_peer(lambda i: remote(SQ, i, sq_buf.at[me], sq_buf.at[me], peer_at(i)).start())
    each_peer(
        lambda i: remote(SQ, i, sq_buf.at[me], sq_buf.at[source_at(i)], peer_at(i)).wait_recv()
    )
    squares = jnp.sum(sq_buf[...], axis=0)[:, :1]
    scaling = lax.rsqrt(squares / features + 1e-05)
    normed = (residual * scaling * gain_ref[...].astype(jnp.float32)).astype(jnp.bfloat16)

    wkv_copy.wait()

    def keyval(c, carry):
        at = pl.multiple_of(c * 512, 512)
        kv_part[:, pl.ds(at, 512)] = jnp.dot(
            normed, wkv_v[:, pl.ds(at, 512)], preferred_element_type=jnp.float32
        )
        return carry

    lax.fori_loop(0, kv_part.shape[1] // 512, keyval, 0)

    def project(i, target):
        wq_copy(i).wait()
        wo_copy(i).start()
        at = pl.multiple_of(peer_at(i) // per_unit * HD, HD)
        target[:, :columns] = jnp.dot(normed, wq_v[i], preferred_element_type=jnp.float32)
        target[:, columns:] = kv_part[:, pl.ds(at, HD)]

    def project_send(i):
        project(i, q_send.at[i])
        remote(QKV, i, q_send.at[i], q_recv.at[me], peer_at(i)).start()

    each_peer(project_send)
    kv_copy.start()
    project(0, q_recv.at[me])
    each_peer(
        lambda i: remote(QKV, i, q_send.at[i], q_recv.at[source_at(i)], peer_at(i)).wait_recv()
    )

    total = jnp.sum(q_recv[...], axis=0)
    cosine = cos_ref[...]
    sine = sin_ref[...]

    def rotated(v):
        return v * cosine + pltpu.roll(v, HD // 2, 1) * sine

    units = [rotated(total[:, u * HD : (u + 1) * HD]) for u in range(heads)]
    last = total[:, columns:]
    units.append(jnp.where(me // per_unit < KVH, rotated(last), last))
    while len(units) * rows < gathered.shape[1]:
        units.append(jnp.zeros((rows, HD), jnp.float32))
    gathered[me] = jnp.concatenate(units, axis=0).astype(jnp.bfloat16)
    each_peer(
        lambda i: remote(GATHER, i, gathered.at[me], gathered.at[me], peer_at(i)).start()
    )
    kv_copy.wait()
    each_peer(
        lambda i: remote(
            GATHER, i, gathered.at[me], gathered.at[source_at(i)], peer_at(i)
        ).wait_recv()
    )

    inv_root = HD ** (-0.5)
    q_rows = GROUP * rows
    request_of = lax.broadcasted_iota(jnp.int32, (q_rows, window), 0) % requests
    slot = me * window + lax.broadcasted_iota(jnp.int32, (q_rows, window), 1)
    length_of = jnp.full((q_rows, window), len_ref[0], jnp.int32)
    for r in range(1, requests):
        length_of = jnp.where(request_of == r, len_ref[r], length_of)
    live = slot < length_of
    lane = lax.broadcasted_iota(jnp.int32, (rows, HD), 1)

    def attend(step, carry):
        k = lax.rem(me // per_kv + 1 + step, KVH)
        key_at = pl.multiple_of(k * HD, HD)
        value_at = pl.multiple_of((KVH + k) * HD, HD)
        queries = jnp.concatenate(
            [gathered[k * per_kv + j, :head_rows, :] for j in range(per_kv)], axis=0
        )
        keys = kv_v[:, :, pl.ds(key_at, HD)].reshape(requests * window, HD)
        values = kv_v[:, :, pl.ds(value_at, HD)].reshape(requests * window, HD)
        scores = lax.dot_general(
            queries, keys, (((1,), (1,)), ((), ())), preferred_element_type=jnp.float32
        )
        cached = scores[:, :window]
        for r in range(1, requests):
            cached = jnp.where(
                request_of == r, scores[:, r * window : (r + 1) * window], cached
            )
        cached = jnp.where(live, cached * inv_root, LIVE_MIN)
        top = jnp.max(cached, axis=-1, keepdims=True)
        weights = jnp.where(live, jnp.exp(cached - top), 0.0)
        weights = weights.astype(jnp.bfloat16).astype(jnp.float32)
        weight_total = jnp.sum(weights, axis=-1, keepdims=True)
        spread = jnp.concatenate(
            [jnp.where(request_of == r, weights, 0.0) for r in range(requests)], axis=1
        ).astype(jnp.bfloat16)
        weighted = jnp.dot(spread, values, preferred_element_type=jnp.float32)
        for j in range(per_kv):
            d = k * per_kv + j
            first = j * head_rows
            stats = jnp.zeros((rows, HD), jnp.float32)
            for u in range(heads):
                at = first + u * rows
                stats = jnp.where(lane == u, top[at : at + rows], stats)
                stats = jnp.where(lane == HD // 2 + u, weight_total[at : at + rows], stats)
            block = jnp.concatenate([weighted[first : first + head_rows], stats], axis=0)

            @pl.when(d == me)
            def _():
                o_recv[me] = block

            @pl.when(d != me)
            def _():
                i = lax.rem(d - me + n, n)
                o_send[i] = block
                remote(MERGE, i, o_send.at[i], o_recv.at[me], d).start()

        return carry

    lax.fori_loop(0, KVH, attend, 0)

    my_kv = me // per_kv

    def unit_rows(u):
        return gathered[u * per_unit, head_rows : head_rows + 16, :].astype(jnp.float32)[:rows]

    new_keys = unit_rows(my_kv)
    new_values = unit_rows(KVH + my_kv)
    earlier_keys = pltpu.roll(new_keys, requests, 0)
    earlier_values = pltpu.roll(new_values, requests, 0)
    my_queries = gathered[me, :head_rows, :].astype(jnp.float32)
    second = lax.broadcasted_iota(jnp.int32, (rows, HD), 0) >= requests
    same = jnp.zeros((rows, HD), jnp.float32)
    earlier = jnp.zeros((rows, HD), jnp.float32)
    for u in range(heads):
        q = my_queries[u * rows : (u + 1) * rows]
        same = jnp.where(lane == u, jnp.sum(q * new_keys, axis=-1, keepdims=True), same)
        earlier = jnp.where(
            lane == u, jnp.sum(q * earlier_keys, axis=-1, keepdims=True), earlier
        )
    same = same * inv_root
    earlier = jnp.where(second, earlier * inv_root, LIVE_MIN)

    each_peer(
        lambda i: remote(MERGE, i, o_send.at[i], o_recv.at[source_at(i)], peer_at(i)).wait_recv()
    )
    stats = [o_recv[d, head_rows:, :] for d in range(n)]
    top = jnp.maximum(same, earlier)
    for d in range(n):
        top = jnp.maximum(top, stats[d])
    same_weight = jnp.exp(same - top).astype(jnp.bfloat16).astype(jnp.float32)
    earlier_weight = jnp.exp(earlier - top).astype(jnp.bfloat16).astype(jnp.float32)
    denominator = same_weight + earlier_weight
    numerators = [
        same_weight[:, u : u + 1] * new_values + earlier_weight[:, u : u + 1] * earlier_values
        for u in range(heads)
    ]
    for d in range(n):
        rescale = jnp.exp(stats[d] - top)
        denominator += rescale * pltpu.roll(stats[d], HD // 2, 1)
        for u in range(heads):
            numerators[u] += rescale[:, u : u + 1] * o_recv[d, u * rows : (u + 1) * rows, :]
    attended = jnp.concatenate(
        [numerators[u] / denominator[:, u : u + 1] for u in range(heads)], axis=1
    ).astype(jnp.bfloat16)

    half = width // 2

    def output(i, target):
        wo_copy(i).wait()
        y = jnp.dot(attended, wo_v[i], preferred_element_type=jnp.float32)
        target[...] = jnp.concatenate([y[:, :half], y[:, half:]], axis=0).astype(jnp.bfloat16)

    def output_send(i):
        output(i, p_send.at[i])
        remote(PROJ, i, p_send.at[i], p_recv.at[me], peer_at(i)).start()

    each_peer(output_send)
    output(0, p_recv.at[me])
    each_peer(
        lambda i: remote(PROJ, i, p_send.at[i], p_recv.at[source_at(i)], peer_at(i)).wait_recv()
    )
    summed = jnp.sum(p_recv[...].astype(jnp.float32), axis=0)
    summed = residual + jnp.concatenate([summed[:rows], summed[rows:]], axis=1)
    for s in range(steps):
        out_ref[s] = summed[s * requests : (s + 1) * requests].astype(jnp.bfloat16)

    def drain(i):
        remote(SQ, i, sq_buf.at[me], sq_buf.at[me], peer_at(i)).wait_send()
        remote(QKV, i, q_send.at[i], q_recv.at[me], peer_at(i)).wait_send()
        remote(GATHER, i, gathered.at[me], gathered.at[me], peer_at(i)).wait_send()
        remote(MERGE, i, o_send.at[i], o_recv.at[me], peer_at(i)).wait_send()
        remote(PROJ, i, p_send.at[i], p_recv.at[me], peer_at(i)).wait_send()

    each_peer(drain)


def on_device(n, residual, norm_gain, w_query, w_keyval, w_out, kv_cache, lengths):
    steps, requests, width = residual.shape
    rows = steps * requests
    heads = QH // n
    columns = heads * HD
    halfway = HD // 2
    position = lengths[None, :] + jnp.arange(steps, dtype=jnp.int32)[:, None]
    frequency = 500000.0 ** (-2.0 * jnp.arange(halfway, dtype=jnp.float32) / HD)
    angles = position.reshape(rows, 1).astype(jnp.float32) * frequency
    cosine = jnp.cos(angles)
    sine = jnp.sin(angles)
    cosine = jnp.concatenate([cosine, cosine], axis=-1)
    sine = jnp.concatenate([-sine, sine], axis=-1)

    gather_rows = ((heads + 1) * rows + 15) // 16 * 16
    vmem = pl.BlockSpec(memory_space=pltpu.VMEM)
    anywhere = pl.BlockSpec(memory_space=pl.ANY)
    bf16 = jnp.bfloat16
    f32 = jnp.float32
    return pl.pallas_call(
        functools.partial(kernel, n),
        out_shape=jax.ShapeDtypeStruct((steps, requests, width), bf16),
        in_specs=[pl.BlockSpec(memory_space=pltpu.SMEM), vmem, vmem, vmem, vmem]
        + [anywhere] * 4,
        out_specs=vmem,
        scratch_shapes=[
            pltpu.VMEM((n, width, columns), bf16),
            pltpu.VMEM(w_keyval.shape, bf16),
            pltpu.VMEM((n, w_out.shape[0], width), bf16),
            pltpu.VMEM(kv_cache.shape, bf16),
            pltpu.VMEM((n, rows, HD), f32),
            pltpu.VMEM((rows, w_keyval.shape[1]), f32),
            pltpu.VMEM((n, rows, columns + HD), f32),
            pltpu.VMEM((n, rows, columns + HD), f32),
            pltpu.VMEM((n, gather_rows, HD), bf16),
            pltpu.VMEM((n, (heads + 1) * rows, HD), f32),
            pltpu.VMEM((n, (heads + 1) * rows, HD), f32),
            pltpu.VMEM((n, 2 * rows, width // 2), bf16),
            pltpu.VMEM((n, 2 * rows, width // 2), bf16),
            pltpu.SemaphoreType.DMA((n,)),
            pltpu.SemaphoreType.DMA,
            pltpu.SemaphoreType.DMA((n,)),
            pltpu.SemaphoreType.DMA,
            pltpu.SemaphoreType.DMA((5, n)),
            pltpu.SemaphoreType.DMA((5, n)),
        ],
        compiler_params=pltpu.CompilerParams(
            collective_id=0, has_side_effects=True, vmem_limit_bytes=56 * 2**20
        ),
    )(lengths, residual, norm_gain.reshape(1, width), cosine, sine, w_query, w_keyval, w_out, kv_cache)


def solution(mesh):
    placed = (
        P(None, "groups", "tp"),
        P("tp"),
        P("tp", None),
        P("tp", None),
        P("tp", None),
        P("groups", "tp", None),
        P("groups"),
    )
    return jax.shard_map(
        functools.partial(on_device, mesh.shape["tp"]),
        mesh=mesh,
        in_specs=placed,
        out_specs=P(None, "groups", "tp"),
        check_vma=False,
    )
```

time: 410 us -> 52.7 us (0.13)
  waiting for transfers between devices: 185 us -> 0 us
  blocking collectives: 125 us -> 0 us
  local copies, waits for them, and re-layouts: 59 us -> 2.69 us
  Pallas kernels: 0 us -> 48.2 us
  matrix products: 20.9 us -> 0 us
  between operations: 13.3 us -> 0.01 us
    unnamed x5 -> x0, waiting for transfers between devices: 111 us -> none
    psum x1 -> x0, waiting for transfers between devices: 74.2 us -> none  [on_device(): query_total, keyval_total = lax.psum((query_part, keyval_part), 'tp')]
    psum x2 -> x0, blocking collectives: 64.6 us -> none  [the longest x1 34.9 us: on_device(): squares = lax.psum(jnp.sum(wide_residual * wide_residual, axis=-1), 'tp')]
    pmax x1 -> x0, blocking collectives: 60.5 us -> none  [on_device(): cache_top = lax.pmax(local_top, 'tp')]
    unnamed x20 -> x1, local copies, waits for them, and re-layouts: 52.5 us -> 1.33 us
    pallas_call x0 -> x1, Pallas kernels: none -> 48.2 us  [on_device(): pl.pallas_call(functools.partial(kernel, n), out_shape=jax.ShapeDtypeStru...]
    dot_general x7 -> x0, matrix products: 20.9 us -> none  [the longest x1 8.2 us: on_device(): query_part = jnp.dot(flat_rows, w_query, preferred_element_type=jnp.float32)]
    slice x1 -> x0, local copies, waits for them, and re-layouts: 4.65 us -> none  [on_device(): cache_values = kv_cache[:, :, KVH * HD:].reshape(row_count, window, KVH, HD)]
  transfers between devices with their start and end apart: 3 -> 0, of which waited for: 3 -> 0; matrix products, arithmetic and copies ran while one was open for 3% -> 0% of each run, Pallas kernels for 0% -> 0%
where the time goes in v1:
time: 52.7 us; the launch traced here: 52.4 us
  Pallas kernels  48.2 us (91%)
  local copies, waits for them, and re-layouts  2.69 us (5%)
  other arithmetic  1.46 us (3%)
    pallas_call x1, Pallas kernels, on_device(): pl.pallas_call(functools.partial(kernel, n), out_shape=jax.ShapeDtypeStru...  48.2 us
    unnamed x1, local copies, waits for them, and re-layouts  1.33 us
    reshape x1, local copies, waits for them, and re-layouts, on_device(): norm_gain.reshape(1, width)  1.28 us

profile of v1, /device:TPU:0, one launch (start us, length us, event | category | flops | bytes accessed | tf_op | source)
XLA Modules:
  0.0 52.4 jit_solution(9065638197542682555)
XLA Ops:
  0.0 0.7 %add_convert_fusion = f32[2,4]{1,0:T(2,128)S(1)} fusion(s32[4]{0:T(128)} %len_ref.1), kind=kLoop, calls=%fused_computation.4 | loop fusion | flops 16 | bytes 48 | tf_op jit(solution)/shard_map/convert_element_type | solution.py:290
  0.7 0.1 convert_element_type.12
  0.8 1.3 %reshape.26.gain_ref = bf16[1,1024]{1,0:T(2,128)(2,1)} reshape(bf16[1024]{0:T(1024)(128)(2,1)} %param.8) | data formatting | bytes 4096 | tf_op jit(solution)/shard_map/reshape | solution.py:331
  2.0 0.1 fusion
  2.1 0.7 %pad_maximum_fusion = (f32[8,128]{1,0:T(8,128)}, f32[8,128]{1,0:T(8,128)}) fusion(f32[8,64]{1,0:T(8,128)S(1)} %get-tuple-element.7, f32[8,64]{1,0:T(8,128)S(1)} %get-tuple-element.6, f32[8,64]{1,0:T(8,128)S(1)} %get-tuple-element.5), kind=kLoop, calls=%fused_computation.2 | loop fusion | flops 2048 | bytes 14336 | tf_op jit(solution)/shard_map/concatenate | solution.py:293
  2.8 48.2 %shard_map.73 = bf16[2,4,1024]{2,1,0:T(4,128)(2,1)} custom-call(s32[4]{0:T(128)} %len_ref.1, bf16[2,4,1024]{2,1,0:T(4,128)(2,1)} %res_ref.1, bf16[1,1024]{1,0:T(2,128)(2,1)} %reshape.26.gain_ref, f32[8,128]{1,0:T(8,128)} %get-tuple-element.8.cos_ref, f32[8,128]{1,0:T(8,128)} %get-tuple-element.9.sin_ref, bf16[1024,8192]{1,0:T(8,128)(2,1)} %wq_hbm.1, ...), custom_call_target="tpu_custom_call" | custom-call | tf_op jit(solution)/shard_map/pallas_call | solution.py:301
  51.1 1.3 %copy.9 = bf16[2,4,1024]{2,1,0:T(4,128)(2,1)} copy(bf16[2,4,1024]{2,1,0:T(4,128)(2,1)} %shard_map.73) | data formatting | bytes 32768
  (1 shorter events, 0.0 us)

commit v2 on v1

v2 whole, which is shorter than its diff:
```python
import functools

import jax
import jax.numpy as jnp
from jax import lax
from jax.experimental import pallas as pl
from jax.experimental.pallas import tpu as pltpu
from jax.sharding import PartitionSpec as P

QH = 64
KVH = 8
HD = 128
UNITS = 2 * KVH
GROUP = QH // KVH
LIVE_MIN = -1e30
MESH = pl.DeviceIdType.MESH
SQ, QKV, GATHER, MERGE, PROJ = range(5)


def kernel(
    n,
    len_ref, res_ref, gain_ref, freq_ref, wq_hbm, wkv_hbm, wo_hbm, kv_hbm,
    out_ref,
    wq_v, wkv_v, wo_v, kv_v, sq_pair, sq_buf, kv_part,
    q_own, q_other, q_mate, q_recv, gathered,
    o_own, o_other, o_mate, o_recv, p_own, p_other, p_mate, p_recv,
    wq_sem, wkv_sem, wo_sem, kv_sem, send_sem, recv_sem,
):
    steps, requests, width = res_ref.shape
    rows = steps * requests
    window = kv_hbm.shape[1]
    features = width * n
    heads = QH // n
    columns = heads * HD
    head_rows = heads * rows
    per_kv = n // KVH
    per_unit = n // UNITS
    chips = n // 2
    me = lax.axis_index("tp")
    core = lax.rem(me, 2)
    chip = me // 2
    mate = me + 1 - 2 * core

    def chip_at(i):
        return lax.rem(chip + i, chips)

    def source_at(i):
        return lax.rem(chip - i + chips, chips)

    def peer_at(i):
        return chip_at(i) * 2 + core

    def across(phase, i, src, dst):
        return pltpu.make_async_remote_copy(
            src_ref=src,
            dst_ref=dst,
            send_sem=send_sem.at[phase, i],
            recv_sem=recv_sem.at[phase, i],
            device_id={"tp": peer_at(i)},
            device_id_type=MESH,
        )

    def to_mate(phase, i, src, dst):
        return pltpu.make_async_remote_copy(
            src_ref=src,
            dst_ref=dst,
            send_sem=send_sem.at[phase, chips + i],
            recv_sem=recv_sem.at[phase, chips + i],
            device_id={"tp": mate},
            device_id_type=MESH,
        )

    def each_peer(body):
        lax.fori_loop(1, chips, lambda i, c: (body(i), c)[1], 0)

    def each_chip(body):
        each_peer(body)
        body(0)

    def staggered(work, send):
        work(1)

        def both(i, carry):
            work(i)
            send(i - 1)
            return carry

        lax.fori_loop(2, chips, both, 0)
        work(0)
        send(chips - 1)

    def wq_copy(i):
        at = pl.multiple_of(chip_at(i) * (2 * columns), 2 * columns)
        return pltpu.make_async_copy(
            wq_hbm.at[:, pl.ds(at, 2 * columns)], wq_v.at[i], wq_sem.at[i]
        )

    def wo_copy(i):
        at = pl.multiple_of(chip_at(i) * (2 * width), 2 * width)
        return pltpu.make_async_copy(wo_hbm.at[:, pl.ds(at, 2 * width)], wo_v.at[i], wo_sem.at[i])

    wkv_copy = pltpu.make_async_copy(wkv_hbm, wkv_v, wkv_sem)
    kv_copy = pltpu.make_async_copy(kv_hbm, kv_v, kv_sem)

    barrier = pltpu.get_barrier_semaphore()
    pl.semaphore_signal(barrier, inc=1, device_id={"tp": mate}, device_id_type=MESH)
    each_peer(
        lambda i: pl.semaphore_signal(
            barrier, inc=1, device_id={"tp": peer_at(i)}, device_id_type=MESH
        )
    )
    wkv_copy.start()
    each_chip(lambda i: wq_copy(i).start())
    kv_copy.start()
    each_chip(lambda i: wo_copy(i).start())

    residual = jnp.concatenate(
        [res_ref[s].astype(jnp.float32) for s in range(steps)], axis=0
    )
    lane = lax.broadcasted_iota(jnp.int32, (rows, HD), 1)
    diagonal = lane == lax.broadcasted_iota(jnp.int32, (rows, HD), 0)
    own_squares = jnp.sum(residual * residual, axis=-1, keepdims=True)
    sq_pair[core] = jnp.sum(jnp.where(diagonal, own_squares, 0.0), axis=0, keepdims=True)
    row = lax.broadcasted_iota(jnp.int32, (rows, HD), 0)
    position = jnp.full((rows, HD), len_ref[0], jnp.int32)
    for r in range(1, requests):
        position = jnp.where(row % requests == r, len_ref[r], position)
    position = position + row // requests
    angles = position.astype(jnp.float32) * freq_ref[...]
    cosine = jnp.cos(angles)
    sine = jnp.sin(angles)
    sine = jnp.where(lane < HD // 2, -sine, sine)
    pl.semaphore_wait(barrier, chips)

    to_mate(SQ, 0, sq_pair.at[core], sq_pair.at[core]).start()
    to_mate(SQ, 0, sq_pair.at[core], sq_pair.at[1 - core]).wait_recv()
    sq_buf[chip] = sq_pair[0] + sq_pair[1]
    each_peer(lambda i: across(SQ, i, sq_buf.at[chip], sq_buf.at[chip]).start())
    each_peer(lambda i: across(SQ, i, sq_buf.at[chip], sq_buf.at[source_at(i)]).wait_recv())
    squares = jnp.sum(
        jnp.where(diagonal, jnp.sum(sq_buf[...], axis=0), 0.0), axis=-1, keepdims=True
    )
    scaling = lax.rsqrt(squares / features + 1e-05)
    normed = (residual * scaling * gain_ref[...].astype(jnp.float32).reshape(1, width)).astype(jnp.bfloat16)

    wkv_copy.wait()

    def keyval(c, carry):
        at = pl.multiple_of(c * 512, 512)
        kv_part[:, pl.ds(at, 512)] = jnp.dot(
            normed, wkv_v[:, pl.ds(at, 512)], preferred_element_type=jnp.float32
        )
        return carry

    lax.fori_loop(0, kv_part.shape[1] // 512, keyval, 0)

    def project(i):
        wq_copy(i).wait()
        y = jnp.dot(normed, wq_v[i], preferred_element_type=jnp.float32)
        first, second = y[:, :columns], y[:, columns:]
        for target, c in ((q_other, 1 - core), (q_own, core)):
            at = pl.multiple_of((chip_at(i) * 2 + c) // per_unit * HD, HD)
            target[i, :, :columns] = jnp.where(c == 0, first, second)
            target[i, :, columns:] = kv_part[:, pl.ds(at, HD)]
        to_mate(QKV, i, q_other.at[i], q_mate.at[i]).start()

    def project_send(i):
        to_mate(QKV, i, q_other.at[i], q_mate.at[i]).wait_recv()
        q_own[i] = q_own[i] + q_mate[i]
        across(QKV, i, q_own.at[i], q_recv.at[chip]).start()

    staggered(project, project_send)
    to_mate(QKV, 0, q_other.at[0], q_mate.at[0]).wait_recv()
    q_recv[chip] = q_own[0] + q_mate[0]
    each_peer(lambda i: across(QKV, i, q_own.at[i], q_recv.at[source_at(i)]).wait_recv())

    total = jnp.sum(q_recv[...], axis=0)

    def rotated(v):
        return v * cosine + pltpu.roll(v, HD // 2, 1) * sine

    units = [rotated(total[:, u * HD : (u + 1) * HD]) for u in range(heads)]
    last = total[:, columns:]
    units.append(jnp.where(me // per_unit < KVH, rotated(last), last))
    while len(units) * rows < gathered.shape[1]:
        units.append(jnp.zeros((rows, HD), jnp.float32))
    gathered[me] = jnp.concatenate(units, axis=0).astype(jnp.bfloat16)
    each_peer(lambda i: across(GATHER, i, gathered.at[me], gathered.at[me]).start())
    to_mate(GATHER, 0, gathered.at[me], gathered.at[me]).start()

    def forward(i):
        block = gathered.at[source_at(i) * 2 + core]
        across(GATHER, i, gathered.at[me], block).wait_recv()
        to_mate(GATHER, i, block, block).start()

    each_peer(forward)
    kv_copy.wait()

    def from_mate(i):
        block = gathered.at[source_at(i) * 2 + 1 - core]
        to_mate(GATHER, i, gathered.at[me], block).wait_recv()

    each_chip(from_mate)

    inv_root = HD ** (-0.5)
    q_rows = GROUP * rows
    request_of = lax.broadcasted_iota(jnp.int32, (q_rows, window), 0) % requests
    slot = me * window + lax.broadcasted_iota(jnp.int32, (q_rows, window), 1)
    length_of = jnp.full((q_rows, window), len_ref[0], jnp.int32)
    for r in range(1, requests):
        length_of = jnp.where(request_of == r, len_ref[r], length_of)
    live = slot < length_of

    def attend(step, carry):
        k = lax.rem(me // per_kv + 1 + step, KVH)
        key_at = pl.multiple_of(k * HD, HD)
        value_at = pl.multiple_of((KVH + k) * HD, HD)
        queries = jnp.concatenate(
            [gathered[k * per_kv + j, :head_rows, :] for j in range(per_kv)], axis=0
        )
        keys = kv_v[:, :, pl.ds(key_at, HD)].reshape(requests * window, HD)
        values = kv_v[:, :, pl.ds(value_at, HD)].reshape(requests * window, HD)
        scores = lax.dot_general(
            queries, keys, (((1,), (1,)), ((), ())), preferred_element_type=jnp.float32
        )
        cached = scores[:, :window]
        for r in range(1, requests):
            cached = jnp.where(
                request_of == r, scores[:, r * window : (r + 1) * window], cached
            )
        cached = jnp.where(live, cached * inv_root, LIVE_MIN)
        top = jnp.max(cached, axis=-1, keepdims=True)
        weights = jnp.where(live, jnp.exp(cached - top), 0.0)
        weights = weights.astype(jnp.bfloat16).astype(jnp.float32)
        weight_total = jnp.sum(weights, axis=-1, keepdims=True)
        spread = jnp.concatenate(
            [jnp.where(request_of == r, weights, 0.0) for r in range(requests)], axis=1
        ).astype(jnp.bfloat16)
        weighted = jnp.dot(spread, values, preferred_element_type=jnp.float32)
        blocks = []
        for j in range(per_kv):
            first = j * head_rows
            stats = jnp.zeros((rows, HD), jnp.float32)
            for u in range(heads):
                at = first + u * rows
                stats = jnp.where(lane == u, top[at : at + rows], stats)
                stats = jnp.where(lane == HD // 2 + u, weight_total[at : at + rows], stats)
            blocks.append(
                jnp.concatenate([weighted[first : first + head_rows], stats], axis=0)
            )
        for j in range(0, per_kv, 2):
            i = lax.rem((k * per_kv + j) // 2 - chip + chips, chips)
            o_own[i] = jnp.where(core == 0, blocks[j], blocks[j + 1])
            o_other[i] = jnp.where(core == 0, blocks[j + 1], blocks[j])
            to_mate(MERGE, i, o_other.at[i], o_mate.at[i]).start()
        return carry

    def merged(i):
        to_mate(MERGE, i, o_other.at[i], o_mate.at[i]).wait_recv()
        one = o_own[i, head_rows:, :]
        two = o_mate[i, head_rows:, :]
        top = jnp.maximum(one, two)
        scale_one = jnp.exp(one - top)
        scale_two = jnp.exp(two - top)
        weight_total = scale_one * pltpu.roll(one, HD // 2, 1) + scale_two * pltpu.roll(
            two, HD // 2, 1
        )
        parts = []
        for u in range(heads):
            at = u * rows
            parts.append(
                scale_one[:, u : u + 1] * o_own[i, at : at + rows, :]
                + scale_two[:, u : u + 1] * o_mate[i, at : at + rows, :]
            )
        parts.append(jnp.where(lane < HD // 2, top, pltpu.roll(weight_total, HD // 2, 1)))
        return jnp.concatenate(parts, axis=0)

    def merge_send(i):
        o_own[i] = merged(i)
        across(MERGE, i, o_own.at[i], o_recv.at[chip]).start()

    if chips == KVH:
        staggered(lambda i: attend(lax.rem(i - 1 + KVH, KVH), 0), merge_send)
    else:
        lax.fori_loop(0, KVH, attend, 0)
        each_peer(merge_send)
    o_recv[chip] = merged(0)

    my_kv = me // per_kv

    def unit_rows(u):
        return gathered[u * per_unit, head_rows : head_rows + 16, :].astype(jnp.float32)[:rows]

    new_keys = unit_rows(my_kv)
    new_values = unit_rows(KVH + my_kv)
    earlier_keys = pltpu.roll(new_keys, requests, 0)
    earlier_values = pltpu.roll(new_values, requests, 0)
    my_queries = gathered[me, :head_rows, :].astype(jnp.float32)
    second = lax.broadcasted_iota(jnp.int32, (rows, HD), 0) >= requests
    same = jnp.zeros((rows, HD), jnp.float32)
    earlier = jnp.zeros((rows, HD), jnp.float32)
    for u in range(heads):
        q = my_queries[u * rows : (u + 1) * rows]
        same = jnp.where(lane == u, jnp.sum(q * new_keys, axis=-1, keepdims=True), same)
        earlier = jnp.where(
            lane == u, jnp.sum(q * earlier_keys, axis=-1, keepdims=True), earlier
        )
    same = same * inv_root
    earlier = jnp.where(second, earlier * inv_root, LIVE_MIN)

    each_peer(lambda i: across(MERGE, i, o_own.at[i], o_recv.at[source_at(i)]).wait_recv())
    stats = [o_recv[d, head_rows:, :] for d in range(chips)]
    top = jnp.maximum(same, earlier)
    for d in range(chips):
        top = jnp.maximum(top, stats[d])
    same_weight = jnp.exp(same - top).astype(jnp.bfloat16).astype(jnp.float32)
    earlier_weight = jnp.exp(earlier - top).astype(jnp.bfloat16).astype(jnp.float32)
    denominator = same_weight + earlier_weight
    numerators = [
        same_weight[:, u : u + 1] * new_values + earlier_weight[:, u : u + 1] * earlier_values
        for u in range(heads)
    ]
    for d in range(chips):
        rescale = jnp.exp(stats[d] - top)
        denominator += rescale * pltpu.roll(stats[d], HD // 2, 1)
        for u in range(heads):
            numerators[u] += rescale[:, u : u + 1] * o_recv[d, u * rows : (u + 1) * rows, :]
    attended = jnp.concatenate(
        [numerators[u] / denominator[:, u : u + 1] for u in range(heads)], axis=1
    ).astype(jnp.bfloat16)

    half = width // 2

    def output(i):
        wo_copy(i).wait()
        y = jnp.dot(attended, wo_v[i], preferred_element_type=jnp.float32)
        first = jnp.concatenate([y[:, :half], y[:, half:width]], axis=0)
        second = jnp.concatenate([y[:, width : width + half], y[:, width + half :]], axis=0)
        p_other[i] = jnp.where(core == 0, second, first).astype(jnp.bfloat16)
        p_own[i] = jnp.where(core == 0, first, second).astype(jnp.bfloat16)
        to_mate(PROJ, i, p_other.at[i], p_mate.at[i]).start()

    def paired(i):
        to_mate(PROJ, i, p_other.at[i], p_mate.at[i]).wait_recv()
        return p_own[i].astype(jnp.float32) + p_mate[i].astype(jnp.float32)

    def output_send(i):
        p_own[i] = paired(i).astype(jnp.bfloat16)
        across(PROJ, i, p_own.at[i], p_recv.at[chip]).start()

    staggered(output, output_send)
    summed = paired(0)
    p_recv[chip] = jnp.zeros(p_recv.shape[1:], jnp.bfloat16)
    each_peer(lambda i: across(PROJ, i, p_own.at[i], p_recv.at[source_at(i)]).wait_recv())
    summed = summed + jnp.sum(p_recv[...].astype(jnp.float32), axis=0)
    summed = jnp.concatenate([summed[:rows], summed[rows:]], axis=1)
    for s in range(steps):
        out_ref[s] = summed[s * requests : (s + 1) * requests]

    to_mate(SQ, 0, sq_pair.at[core], sq_pair.at[core]).wait_send()

    def drain(i):
        across(SQ, i, sq_buf.at[chip], sq_buf.at[chip]).wait_send()
        across(QKV, i, q_own.at[i], q_recv.at[chip]).wait_send()
        across(GATHER, i, gathered.at[me], gathered.at[me]).wait_send()
        across(MERGE, i, o_own.at[i], o_recv.at[chip]).wait_send()
        across(PROJ, i, p_own.at[i], p_recv.at[chip]).wait_send()

    def drain_mate(i):
        to_mate(QKV, i, q_other.at[i], q_mate.at[i]).wait_send()
        to_mate(GATHER, i, gathered.at[me], gathered.at[me]).wait_send()
        to_mate(MERGE, i, o_other.at[i], o_mate.at[i]).wait_send()
        to_mate(PROJ, i, p_other.at[i], p_mate.at[i]).wait_send()

    each_peer(drain)
    each_chip(drain_mate)


def on_device(n, residual, norm_gain, w_query, w_keyval, w_out, kv_cache, lengths):
    steps, requests, width = residual.shape
    rows = steps * requests
    heads = QH // n
    columns = heads * HD
    chips = n // 2
    halfway = HD // 2
    frequency = 500000.0 ** (-2.0 * jnp.arange(halfway, dtype=jnp.float32) / HD)
    frequency = jnp.concatenate([frequency, frequency]).reshape(1, HD)

    gather_rows = ((heads + 1) * rows + 15) // 16 * 16
    vmem = pl.BlockSpec(memory_space=pltpu.VMEM)
    anywhere = pl.BlockSpec(memory_space=pl.ANY)
    bf16 = jnp.bfloat16
    f32 = jnp.float32
    summed = pl.pallas_call(
        functools.partial(kernel, n),
        out_shape=jax.ShapeDtypeStruct((steps, requests, width), f32),
        in_specs=[pl.BlockSpec(memory_space=pltpu.SMEM), vmem, vmem, vmem]
        + [anywhere] * 4,
        out_specs=vmem,
        scratch_shapes=[
            pltpu.VMEM((chips, width, 2 * columns), bf16),
            pltpu.VMEM(w_keyval.shape, bf16),
            pltpu.VMEM((chips, w_out.shape[0], 2 * width), bf16),
            pltpu.VMEM(kv_cache.shape, bf16),
            pltpu.VMEM((2, 1, HD), f32),
            pltpu.VMEM((chips, 1, HD), f32),
            pltpu.VMEM((rows, w_keyval.shape[1]), f32),
        ]
        + [pltpu.VMEM((chips, rows, columns + HD), f32)] * 4
        + [pltpu.VMEM((n, gather_rows, HD), bf16)]
        + [pltpu.VMEM((chips, (heads + 1) * rows, HD), f32)] * 4
        + [pltpu.VMEM((chips, 2 * rows, width // 2), bf16)] * 4
        + [
            pltpu.SemaphoreType.DMA((chips,)),
            pltpu.SemaphoreType.DMA,
            pltpu.SemaphoreType.DMA((chips,)),
            pltpu.SemaphoreType.DMA,
            pltpu.SemaphoreType.DMA((5, n)),
            pltpu.SemaphoreType.DMA((5, n)),
        ],
        compiler_params=pltpu.CompilerParams(
            collective_id=0, has_side_effects=True, vmem_limit_bytes=56 * 2**20
        ),
    )(lengths, residual, norm_gain, frequency, w_query, w_keyval, w_out, kv_cache)
    return (residual.astype(f32) + summed).astype(bf16)


def solution(mesh):
    placed = (
        P(None, "groups", "tp"),
        P("tp"),
        P("tp", None),
        P("tp", None),
        P("tp", None),
        P("groups", "tp", None),
        P("groups"),
    )
    return jax.shard_map(
        functools.partial(on_device, mesh.shape["tp"]),
        mesh=mesh,
        in_specs=placed,
        out_specs=P(None, "groups", "tp"),
        check_vma=False,
    )
```

time: 52.7 us -> 47.2 us (0.90)
  Pallas kernels: 48.2 us -> 44.9 us
  local copies, waits for them, and re-layouts: 2.69 us -> 0.01 us
    pallas_call x1, Pallas kernels: 48.2 us -> 44.9 us  [on_device(): pl.pallas_call(functools.partial(kernel, n), out_shape=jax.ShapeDtypeStru...]
    unnamed x1 -> x2, local copies, waits for them, and re-layouts: 1.33 us -> 0.01 us
    reshape x1 -> x0, local copies, waits for them, and re-layouts: 1.28 us -> none  [on_device(): norm_gain.reshape(1, width)]
    convert_element_type x1, other arithmetic: 0.66 us -> 1.37 us  [on_device(): return (residual.astype(f32) + summed).astype(bf16)]
    concatenate x1 -> x0, other arithmetic: 0.67 us -> none  [on_device(): cosine = jnp.concatenate([cosine, cosine], axis=-1)]
    reshape x0 -> x1, other arithmetic: none -> 0.59 us  [on_device(): frequency = jnp.concatenate([frequency, frequency]).reshape(1, HD)]
where the time goes in v2:
time: 47.2 us; the launch traced here: 46.9 us
  Pallas kernels  44.9 us (95%)
  other arithmetic  1.98 us (4%)
    pallas_call x1, Pallas kernels, on_device(): pl.pallas_call(functools.partial(kernel, n), out_shape=jax.ShapeDtypeStru...  44.9 us
    convert_element_type x1, other arithmetic, on_device(): return (residual.astype(f32) + summed).astype(bf16)  1.37 us

profile of v2, /device:TPU:0, one launch (start us, length us, event | category | flops | bytes accessed | tf_op | source)
XLA Modules:
  0.0 46.9 jit_solution(1753882759958043749)
XLA Ops:
  0.0 0.6 %maximum_bitcast_fusion.freq_ref = f32[1,128]{1,0:T(1,128)} fusion(f32[64]{0:T(128)S(1)} %multiply_power_fusion), kind=kLoop, calls=%fused_computation.1 | loop fusion | flops 128 | bytes 768 | tf_op jit(solution)/shard_map/reshape | solution.py:387
  0.6 0.0 copy-start
  0.6 44.9 %shard_map.73 = f32[2,4,1024]{2,1,0:T(4,128)} custom-call(s32[4]{0:T(128)} %len_ref.1, bf16[2,4,1024]{2,1,0:T(4,128)(2,1)} %res_ref.1, bf16[1024]{0:T(1024)(128)(2,1)} %gain_ref.1, f32[1,128]{1,0:T(1,128)} %maximum_bitcast_fusion.freq_ref, bf16[1024,8192]{1,0:T(8,128)(2,1)} %wq_hbm.1, bf16[1024,2048]{1,0:T(8,128)(2,1)} %wkv_hbm.1, ...), custom_call_target="tpu_custom_call" | custom-call | tf_op jit(solution)/shard_map/pallas_call | solution.py:394
  45.5 0.0 copy-done
  45.6 1.4 %add_convert_fusion = bf16[2,4,1024]{2,1,0:T(4,128)(2,1)} fusion(f32[2,4,1024]{2,1,0:T(4,128)} %shard_map.73, bf16[2,4,1024]{2,1,0:T(4,128)(2,1)S(1)} %copy-done), kind=kLoop, calls=%fused_computation | loop fusion | flops 24576 | bytes 65536 | tf_op jit(solution)/shard_map/convert_element_type | solution.py:425
  (1 shorter events, 0.0 us)
Async XLA Ops:
  0.6 44.9 %copy-start = (bf16[2,4,1024]{2,1,0:T(4,128)(2,1)S(1)}, bf16[2,4,1024]{2,1,0:T(4,128)(2,1)}, u32[]{:S(2)}) copy-start(bf16[2,4,1024]{2,1,0:T(4,128)(2,1)} %res_ref.1) | copy-start | bytes 49156
